TPU v7x, 32 devices: a whole 2x2x4 slice. The times are simulated.
32 devices in a mesh: grp: 4 (over x, core), seq: 8 (over z, y).
Axes of the slice: x: 2, y: 2, z: 4, core: 2. Of those that a mesh axis runs over, the one named last changes fastest.
Arguments:
- signal: bfloat16 [4, 1024, 2048], P('grp', 'seq'), may hold values from -6 to 6
- gate_in: bfloat16 [4, 1024, 2048], P('grp', 'seq'), may hold values from -6 to 6
- gate_out: bfloat16 [4, 1024, 2048], P('grp', 'seq'), may hold values from -6 to 6
- pos_weight: float32 [33, 64], replicated, may hold values from -1 to 1
- pos_bias: float32 [64], replicated, may hold values from -1 to 1
- inner_weight: float32 [2, 64, 64], replicated, may hold values from -0.75 to 0.75
- inner_bias: float32 [2, 64], replicated, may hold values from -1 to 1
- frequency: float32 [64], replicated, may hold values from 1 to 12
- out_weight: float32 [64, 2048], replicated, may hold values from -0.75 to 0.75
- decay_rates: float32 [2048], replicated, may hold values from 0.3 to 3000
- skip_gain: float32 [2048], replicated, may hold values from -6 to 6
Outputs:
- layer_out: bfloat16 [4, 1024, 2048], P('grp', 'seq')
All inputs are finite; a program needn't handle non-finite values.
Results may differ from a plain program's by a relative error of at most 0.009.
Values may be sent and summed in bfloat16 or wider, within the bound.
A program may use at most 64 MiB of HBM per device.

v0:
```python
import jax
import jax.numpy as jnp
from jax import lax
from jax.sharding import PartitionSpec as P

TWO_PI = 6.283185307179586
FLOOR_SHIFT = 0.05
EPSILON = 1e-06
HIGHEST = lax.Precision.HIGHEST


def unit_angle(index, period):
    return (index % period).astype(jnp.float32) * (TWO_PI / period)


def section_tables(row_ids, col_ids, period):
    angle = unit_angle(row_ids[:, None] * col_ids[None, :], period)
    return (jnp.cos(angle).astype(jnp.bfloat16), jnp.sin(angle).astype(jnp.bfloat16))


def filter_hidden(positions, total, pos_weight, pos_bias, inner_weight, inner_bias, frequency):
    band_count = (pos_weight.shape[0] - 1) // 2
    position_f = positions.astype(jnp.float32)
    moments = position_f / (total - 1)
    phases = position_f * (TWO_PI / total)
    tone_list = jnp.linspace(0.0001, band_count - 1, band_count).astype(jnp.float32)
    angles = tone_list[:, None] * phases[None, :]
    features = jnp.concatenate([moments[None, :], jnp.cos(angles), -jnp.sin(angles)], axis=0)
    hidden = jnp.sin(
        frequency[:, None]
        * (jnp.dot(pos_weight.T, features, precision=HIGHEST) + pos_bias[:, None])
    )
    for layer_index in range(inner_weight.shape[0]):
        hidden = jnp.sin(
            frequency[:, None]
            * (
                jnp.dot(inner_weight[layer_index].T, hidden, precision=HIGHEST)
                + inner_bias[layer_index][:, None]
            )
        )
    return (hidden, moments)


def per_device(
    signal,
    gate_in,
    gate_out,
    pos_weight,
    pos_bias,
    inner_weight,
    inner_bias,
    frequency,
    out_weight,
    decay_rates,
    skip_gain,
):
    blocks = lax.axis_size("seq")
    block_id = lax.axis_index("seq")
    span = signal.shape[1]
    width = signal.shape[2]
    rows_freq = 2 * blocks
    length = span * blocks
    period = 2 * length
    gated = (gate_in[0].astype(jnp.float32) * signal[0].astype(jnp.float32)).astype(jnp.bfloat16)
    fwd_cos, fwd_sin = section_tables(
        jnp.arange(rows_freq, dtype=jnp.int32), jnp.arange(blocks, dtype=jnp.int32), rows_freq
    )
    back_cos, back_sin = section_tables(
        jnp.arange(blocks, dtype=jnp.int32), jnp.arange(rows_freq, dtype=jnp.int32), rows_freq
    )
    column_ids = jnp.arange(span, dtype=jnp.int32)
    own = width // blocks
    lanes = lax.all_to_all(gated.T, "seq", split_axis=0, concat_axis=1, tiled=True)
    own_weight = lax.dynamic_slice_in_dim(out_weight, block_id * own, own, 1)
    own_decay = lax.dynamic_slice_in_dim(decay_rates, block_id * own, own, 0)
    hidden, moments = filter_hidden(
        jnp.arange(length, dtype=jnp.int32),
        length,
        pos_weight,
        pos_bias,
        inner_weight,
        inner_bias,
        frequency,
    )
    shaped = jnp.dot(own_weight.T, hidden, precision=HIGHEST) * (
        jnp.exp(-own_decay[:, None] * moments[None, :]) + FLOOR_SHIFT
    )
    own_scale = lax.rsqrt(jnp.sum(shaped * shaped, axis=1) + EPSILON)
    own_taps = shaped.astype(jnp.bfloat16)

    def first_local(source):
        cube = source.reshape(own, blocks, span)
        real_part = jnp.einsum(
            "ca,oab->cob", fwd_cos, cube, preferred_element_type=jnp.float32
        ).astype(jnp.bfloat16)
        imag_part = (
            -jnp.einsum("ca,oab->cob", fwd_sin, cube, preferred_element_type=jnp.float32)
        ).astype(jnp.bfloat16)
        return (real_part, imag_part)

    data_real, data_imag = first_local(lanes)
    taps_real, taps_imag = first_local(own_taps)
    group = 16
    turns = rows_freq // group

    def grouped(array):
        return array.reshape(turns, group, own, span)

    def row_group(pieces):
        row_real, row_imag, tap_real, tap_imag, row_ids = pieces
        wave_ids = row_ids[:, None] + rows_freq * column_ids[None, :]
        angle = unit_angle(wave_ids[:, :, None] * column_ids[None, None, :], period)
        cosines = jnp.cos(angle).astype(jnp.bfloat16)
        sines = jnp.sin(angle).astype(jnp.bfloat16)

        def spectrum_of(part_real, part_imag):
            spec_real = jnp.einsum(
                "rdb,rob->rod", cosines, part_real, preferred_element_type=jnp.float32
            ) + jnp.einsum("rdb,rob->rod", sines, part_imag, preferred_element_type=jnp.float32)
            spec_imag = jnp.einsum(
                "rdb,rob->rod", cosines, part_imag, preferred_element_type=jnp.float32
            ) - jnp.einsum("rdb,rob->rod", sines, part_real, preferred_element_type=jnp.float32)
            return (spec_real, spec_imag)

        wave_real, wave_imag = spectrum_of(row_real, row_imag)
        spec_real, spec_imag = spectrum_of(tap_real, tap_imag)
        filt_real = spec_real.astype(jnp.bfloat16).astype(jnp.float32)
        filt_imag = spec_imag.astype(jnp.bfloat16).astype(jnp.float32)
        lane_scale = own_scale[None, :, None]
        prod_real = ((wave_real * filt_real - wave_imag * filt_imag) * lane_scale).astype(
            jnp.bfloat16
        )
        prod_imag = ((wave_real * filt_imag + wave_imag * filt_real) * lane_scale).astype(
            jnp.bfloat16
        )
        back_real = jnp.einsum(
            "rdb,rod->rob", cosines, prod_real, preferred_element_type=jnp.float32
        ) - jnp.einsum("rdb,rod->rob", sines, prod_imag, preferred_element_type=jnp.float32)
        back_imag = jnp.einsum(
            "rdb,rod->rob", cosines, prod_imag, preferred_element_type=jnp.float32
        ) + jnp.einsum("rdb,rod->rob", sines, prod_real, preferred_element_type=jnp.float32)
        return (back_real.astype(jnp.bfloat16), back_imag.astype(jnp.bfloat16))

    row_list = jnp.arange(rows_freq, dtype=jnp.int32).reshape(turns, group)
    back_real, back_imag = lax.map(
        row_group,
        (grouped(data_real), grouped(data_imag), grouped(taps_real), grouped(taps_imag), row_list),
    )
    back_real = back_real.reshape(rows_freq, own, span)
    back_imag = back_imag.reshape(rows_freq, own, span)
    local_conv = (
        jnp.einsum("ac,cob->oab", back_cos, back_real, preferred_element_type=jnp.float32)
        - jnp.einsum("ac,cob->oab", back_sin, back_imag, preferred_element_type=jnp.float32)
    ) * (1.0 / period)
    returned = lax.all_to_all(
        local_conv.reshape(own, length).astype(jnp.bfloat16),
        "seq",
        split_axis=1,
        concat_axis=0,
        tiled=True,
    ).astype(jnp.float32)
    convolved_rows = returned.T
    mixed = gate_out[0].astype(jnp.float32) * (
        convolved_rows + skip_gain[None, :] * gated.astype(jnp.float32)
    )
    return mixed.astype(jnp.bfloat16)[None]


def solution(mesh):
    return jax.shard_map(
        per_device,
        mesh=mesh,
        in_specs=(
            P("grp", "seq", None),
            P("grp", "seq", None),
            P("grp", "seq", None),
            P(),
            P(),
            P(),
            P(),
            P(),
            P(),
            P(),
            P(),
        ),
        out_specs=P("grp", "seq", None),
        check_vma=False,
    )
```

profile of v0, /device:TPU:0, one launch (start us, length us, event | category | flops | bytes accessed | tf_op | source)
XLA Modules:
  0.0 110.3 jit_solution(9425088088889942498)
XLA Ops:
  0.0 0.0 copy-start
  0.0 1.4 %copy.35 = bf16[1,128,2048]{1,2,0:T(8,128)(2,1)S(1)} copy(bf16[1,128,2048]{2,1,0:T(8,128)(2,1)} %param.12) | data formatting | bytes 1048576 | tf_op args[1]
  1.4 0.0 copy-start.6
  1.4 0.0 copy-start.3
  1.4 0.0 copy-start.5
  1.4 0.0 copy-start.7
  1.4 0.0 copy-start.2
  1.4 1.3 %copy.36 = bf16[1,128,2048]{1,2,0:T(8,128)(2,1)S(1)} copy(bf16[1,128,2048]{2,1,0:T(8,128)(2,1)} %param.11) | data formatting | bytes 1048576 | tf_op args[0]
  2.8 0.9 multiply_convert_fusion
  3.7 7.3 %all-to-all-start = ((bf16[8,256,128]{2,1,0:T(8,128)(2,1)}), bf16[8,256,128]{2,1,0:T(8,128)(2,1)S(1)}, u32[]{:S(2)}, u32[]{:S(2)}) async-start(bf16[8,256,128]{2,1,0:T(8,128)(2,1)} %bitcast.4), calls=%async_computation | async-start | bytes 1048576 | tf_op jit(solution)/shard_map/all_to_all | solution.py:73
  11.1 0.0 copy-done.6
  11.1 0.8 dynamic-slice_negate_fusion
  11.9 0.1 pad_maximum_fusion
  11.9 0.3 multiply_cosine_fusion
  12.2 0.0 copy-done.3
  12.3 0.0 copy-done.5
  12.3 0.0 copy-done.7
  12.3 1.3 %fusion.14 = f32[1024,64]{0,1:T(8,128)S(1)} fusion(f32[33,64]{1,0:T(8,128)S(1)} %copy-done.3, f32[16,1024]{1,0:T(8,128)S(1)} %get-tuple-element.28, f32[16,1024]{1,0:T(8,128)S(1)} %get-tuple-element.27, f32[1,1024]{1,0:T(1,128)S(1)} %convert_multiply_fusion.6, f32[64]{0:T(128)S(1)} %copy-done.7, f32[64]{0:T(128)S(1)} %copy-done.5), kind=kOutput, calls=%fused_computation.36 | convolution fusion | flops 26150912 | bytes 406272 | tf_op jit(solution)/shard_map/dot_general | solution.py:31
  13.6 1.3 %fusion.12 = f32[1024,64]{0,1:T(8,128)S(1)} fusion(f32[1024,64]{0,1:T(8,128)S(1)} %fusion.14, f32[64]{0:T(128)S(1)} %get-tuple-element.40, f32[64]{0:T(128)S(1)} %copy-done.5, f32[2,64,64]{2,1,0:T(8,128)S(1)} %copy-done.2), kind=kOutput, calls=%fused_computation.33 | convolution fusion | flops 50462720 | bytes 558080 | tf_op jit(solution)/shard_map/dot_general | solution.py:37
  14.8 1.3 %fusion.10 = f32[1024,64]{0,1:T(8,128)S(1)} fusion(f32[1024,64]{0,1:T(8,128)S(1)} %fusion.12, f32[64]{0:T(128)S(1)} %get-tuple-element.29, f32[64]{0:T(128)S(1)} %copy-done.5, f32[2,64,64]{2,1,0:T(8,128)S(1)} %copy-done.2), kind=kOutput, calls=%fused_computation.30 | convolution fusion | flops 50462720 | bytes 558080 | tf_op jit(solution)/shard_map/dot_general | solution.py:37
  16.1 1.3 %multiply_reduce_fusion = (f32[256]{0:T(256)S(1)}, bf16[32,8,8,128]{3,1,2,0:T(8,128)(2,1)S(1)}) fusion(f32[1024]{0:T(1024)S(1)} %convert_multiply_fusion.4, f32[256]{0:T(256)S(1)} %dynamic-slice_negate_fusion, f32[1024,64]{0,1:T(8,128)S(1)} %fusion.10, f32[64,2048]{1,0:T(8,128)S(1)} %copy-done, s32[]{:T(128)S(6)} %select_n.57), kind=kOutput, calls=%fused_computation.46 | convolution fusion | flops 202899200 | bytes 858116 | tf_op jit(solution)/shard_map/dot_general | solution.py:85
  17.4 0.1 copy.50
  17.5 0.5 negate_convert_fusion
  18.1 0.5 convolution_convert_fusion
  18.6 5.8 %fusion.26 = f32[16,256,128]{2,1,0:T(8,128)S(1)} fusion(bf16[16,256,128]{2,0,1:T(8,128)(2,1)S(1)} %negate_convert_fusion, s32[16,128]{1,0:T(8,128)S(1)} %iota_add_fusion), kind=kOutput, calls=%fused_computation.53 | convolution fusion | flops 138149888 | bytes 3153920 | tf_op jit(solution)/shard_map/while/body/eval_jaxpr/rdb,rob->rod/dot_general | solution.py:120
  24.4 5.8 %fusion.30 = f32[16,256,128]{2,1,0:T(8,128)S(1)} fusion(bf16[16,256,128]{2,0,1:T(8,128)(2,1)S(1)} %convolution_convert_fusion, s32[16,128]{1,0:T(8,128)S(1)} %iota_add_fusion), kind=kOutput, calls=%fused_computation.57 | convolution fusion | flops 138149888 | bytes 3153920 | tf_op jit(solution)/shard_map/while/body/eval_jaxpr/rdb,rob->rod/dot_general | solution.py:117
  30.2 5.1 %subtract_convert_fusion.1 = bf16[16,256,128]{2,1,0:T(8,128)(2,1)S(1)} fusion(f32[16,256,128]{2,1,0:T(8,128)S(1)} %fusion.26, bf16[16,256,128]{2,0,1:T(8,128)(2,1)S(1)} %convolution_convert_fusion, s32[16,128]{1,0:T(8,128)S(1)} %iota_add_fusion), kind=kOutput, calls=%fused_computation.12 | convolution fusion | flops 139198464 | bytes 4202496 | tf_op jit(solution)/shard_map/while/body/eval_jaxpr/rdb,rob->rod/dot_general | solution.py:122
  35.3 5.1 %add_convert_fusion.1 = bf16[16,256,128]{2,1,0:T(8,128)(2,1)S(1)} fusion(f32[16,256,128]{2,1,0:T(8,128)S(1)} %fusion.30, bf16[16,256,128]{2,0,1:T(8,128)(2,1)S(1)} %negate_convert_fusion, s32[16,128]{1,0:T(8,128)S(1)} %iota_add_fusion), kind=kOutput, calls=%fused_computation.13 | convolution fusion | flops 139198464 | bytes 4202496 | tf_op jit(solution)/shard_map/while/body/eval_jaxpr/rdb,rob->rod/dot_general | solution.py:119
  40.3 0.0 all-to-all-done
  40.3 0.6 convolution_convert_fusion.1
  40.9 5.8 %fusion.36 = f32[16,256,128]{2,1,0:T(8,128)S(1)} fusion(bf16[16,256,128]{2,0,1:T(8,128)(2,1)S(1)} %convolution_convert_fusion.1, s32[16,128]{1,0:T(8,128)S(1)} %iota_add_fusion), kind=kOutput, calls=%fused_computation.63 | convolution fusion | flops 138149888 | bytes 3153920 | tf_op jit(solution)/shard_map/while/body/eval_jaxpr/rdb,rob->rod/dot_general | solution.py:117
  46.7 0.6 negate_convert_fusion.1
  47.3 6.0 %fusion.32 = f32[16,256,128]{2,1,0:T(8,128)S(1)} fusion(bf16[16,256,128]{2,0,1:T(8,128)(2,1)S(1)} %negate_convert_fusion.1, s32[16,128]{1,0:T(8,128)S(1)} %iota_add_fusion), kind=kOutput, calls=%fused_computation.59 | convolution fusion | flops 138149888 | bytes 3153920 | tf_op jit(solution)/shard_map/while/body/eval_jaxpr/rdb,rob->rod/dot_general | solution.py:120
  53.3 5.9 %convolution_add_fusion = f32[16,256,128]{2,1,0:T(8,128)S(1)} fusion(f32[16,256,128]{2,1,0:T(8,128)S(1)} %fusion.36, bf16[16,256,128]{2,0,1:T(8,128)(2,1)S(1)} %negate_convert_fusion.1, s32[16,128]{1,0:T(8,128)S(1)} %iota_add_fusion), kind=kOutput, calls=%fused_computation.17 | convolution fusion | flops 138674176 | bytes 5251072 | tf_op jit(solution)/shard_map/while/body/eval_jaxpr/rdb,rob->rod/dot_general | solution.py:119
  59.2 5.2 %fusion.5 = (bf16[16,256,128]{2,1,0:T(8,128)(2,1)S(1)}, bf16[16,256,128]{2,1,0:T(8,128)(2,1)S(1)}) fusion(bf16[16,256,128]{2,1,0:T(8,128)(2,1)S(1)} %add_convert_fusion.1, f32[16,256,128]{2,1,0:T(8,128)S(1)} %convolution_add_fusion, bf16[16,256,128]{2,1,0:T(8,128)(2,1)S(1)} %subtract_convert_fusion.1, f32[256]{0:T(256)S(1)} %add_rsqrt_fusion, ...), kind=kOutput, calls=%fused_computation.9 | convolution fusion | flops 144965632 | bytes 9446400 | tf_op jit(solution)/shard_map/while/body/eval_jaxpr/rdb,rob->rod/dot_general | solution.py:122
  64.4 5.8 %fusion.40 = f32[16,256,128]{2,1,0:T(8,128)S(1)} fusion(bf16[16,256,128]{2,1,0:T(8,128)(2,1)S(1)} %get-tuple-element.23, s32[16,128]{1,0:T(8,128)S(1)} %iota_add_fusion), kind=kOutput, calls=%fused_computation.68 | convolution fusion | flops 138149888 | bytes 3153920 | tf_op jit(solution)/shard_map/while/body/eval_jaxpr/rdb,rod->rob/dot_general | solution.py:139
  70.2 5.8 %fusion.41 = f32[16,256,128]{2,1,0:T(8,128)S(1)} fusion(bf16[16,256,128]{2,1,0:T(8,128)(2,1)S(1)} %get-tuple-element.24, s32[16,128]{1,0:T(8,128)S(1)} %iota_add_fusion), kind=kOutput, calls=%fused_computation.69 | convolution fusion | flops 138149888 | bytes 3153920 | tf_op jit(solution)/shard_map/while/body/eval_jaxpr/rdb,rod->rob/dot_general | solution.py:136
  75.9 4.9 %add_convert_fusion = bf16[16,256,128]{2,1,0:T(8,128)(2,1)S(1)} fusion(f32[16,256,128]{2,1,0:T(8,128)S(1)} %fusion.40, bf16[16,256,128]{2,1,0:T(8,128)(2,1)S(1)} %get-tuple-element.24, s32[16,128]{1,0:T(8,128)S(1)} %iota_add_fusion), kind=kOutput, calls=%fused_computation.10 | convolution fusion | flops 139198464 | bytes 4202496 | tf_op jit(solution)/shard_map/while/body/eval_jaxpr/rdb,rod->rob/dot_general | solution.py:141
  80.8 4.9 %subtract_convert_fusion = bf16[16,256,128]{2,1,0:T(8,128)(2,1)S(1)} fusion(f32[16,256,128]{2,1,0:T(8,128)S(1)} %fusion.41, bf16[16,256,128]{2,1,0:T(8,128)(2,1)S(1)} %get-tuple-element.23, s32[16,128]{1,0:T(8,128)S(1)} %iota_add_fusion), kind=kOutput, calls=%fused_computation.11 | convolution fusion | flops 139198464 | bytes 4202496 | tf_op jit(solution)/shard_map/while/body/eval_jaxpr/rdb,rod->rob/dot_general | solution.py:138
  85.7 0.7 fusion.21
  86.4 0.7 fusion.8
  87.1 0.0 copy-start.4
  87.1 0.9 copy.48
  88.0 6.0 %all-to-all-start.1 = ((bf16[256,8,128]{2,0,1:T(8,128)(2,1)}), bf16[256,8,128]{2,0,1:T(8,128)(2,1)S(1)}, u32[]{:S(2)}, u32[]{:S(2)}) async-start(bf16[256,8,128]{2,0,1:T(8,128)(2,1)} %copy.48), calls=%async_computation.1 | async-start | bytes 1048576 | tf_op jit(solution)/shard_map/all_to_all | solution.py:155
  94.0 0.3 copy.34
  94.2 13.7 %all-to-all-done.1 = bf16[256,8,128]{2,0,1:T(8,128)(2,1)S(1)} async-done(((bf16[256,8,128]{2,0,1:T(8,128)(2,1)}), bf16[256,8,128]{2,0,1:T(8,128)(2,1)S(1)}, u32[]{:S(2)}, u32[]{:S(2)}) %all-to-all-start.1) | async-done | bytes 524320 | tf_op jit(solution)/shard_map/all_to_all | solution.py:155
  107.9 1.4 %fusion.19 = bf16[128,2048]{0,1:T(8,128)(2,1)S(1)} fusion(bf16[1,128,2048]{1,2,0:T(8,128)(2,1)S(1)} %copy.34, bf16[1,128,2048]{1,2,0:T(8,128)(2,1)} %multiply_convert_fusion, f32[2048]{0:T(1024)S(1)} %copy-done.4, bf16[256,8,128]{2,0,1:T(8,128)(2,1)S(1)} %all-to-all-done.1), kind=kLoop, calls=%fused_computation.42 | loop fusion | flops 1835008 | bytes 2105344 | tf_op jit(solution)/shard_map/convert_element_type | solution.py:166
  109.3 1.0 copy.49
  (13 shorter events, 0.1 us)
Async XLA Ops:
  0.0 16.1 %copy-start = (f32[64,2048]{1,0:T(8,128)S(1)}, f32[64,2048]{1,0:T(8,128)}, u32[]{:S(2)}) copy-start(f32[64,2048]{1,0:T(8,128)} %param.19) | copy-start | bytes 1572868
  1.4 9.7 %copy-start.6 = (f32[2,64]{1,0:T(2,128)S(1)}, f32[2,64]{1,0:T(2,128)}, u32[]{:S(2)}) copy-start(f32[2,64]{1,0:T(2,128)} %param.17) | copy-start | bytes 1540
  1.4 10.9 %copy-start.3 = (f32[33,64]{1,0:T(8,128)S(1)}, f32[33,64]{1,0:T(8,128)}, u32[]{:S(2)}) copy-start(f32[33,64]{1,0:T(8,128)} %param.14) | copy-start | bytes 25348
  1.4 10.9 %copy-start.5 = (f32[64]{0:T(128)S(1)}, f32[64]{0:T(128)}, u32[]{:S(2)}) copy-start(f32[64]{0:T(128)} %param.18) | copy-start | bytes 772
  1.4 10.9 %copy-start.7 = (f32[64]{0:T(128)S(1)}, f32[64]{0:T(128)}, u32[]{:S(2)}) copy-start(f32[64]{0:T(128)} %param.15) | copy-start | bytes 772
  1.4 12.1 %copy-start.2 = (f32[2,64,64]{2,1,0:T(8,128)S(1)}, f32[2,64,64]{2,1,0:T(8,128)}, u32[]{:S(2)}) copy-start(f32[2,64,64]{2,1,0:T(8,128)} %param.16) | copy-start | bytes 98308
  3.7 36.6 %all-to-all-start = ((bf16[8,256,128]{2,1,0:T(8,128)(2,1)}), bf16[8,256,128]{2,1,0:T(8,128)(2,1)S(1)}, u32[]{:S(2)}, u32[]{:S(2)}) async-start(bf16[8,256,128]{2,1,0:T(8,128)(2,1)} %bitcast.4), calls=%async_computation | async-start | bytes 1048576 | tf_op jit(solution)/shard_map/all_to_all | solution.py:73
  86.4 7.6 %copy-start.1 = (bf16[1,128,2048]{2,1,0:T(8,128)(2,1)S(1)}, bf16[1,128,2048]{2,1,0:T(8,128)(2,1)}, u32[]{:S(2)}) copy-start(bf16[1,128,2048]{2,1,0:T(8,128)(2,1)} %param.13) | copy-start | bytes 1572868
  87.1 20.8 %copy-start.4 = (f32[2048]{0:T(1024)S(1)}, f32[2048]{0:T(1024)}, u32[]{:S(2)}) copy-start(f32[2048]{0:T(1024)} %param.21) | copy-start | bytes 24580
  88.0 19.9 %all-to-all-start.1 = ((bf16[256,8,128]{2,0,1:T(8,128)(2,1)}), bf16[256,8,128]{2,0,1:T(8,128)(2,1)S(1)}, u32[]{:S(2)}, u32[]{:S(2)}) async-start(bf16[256,8,128]{2,0,1:T(8,128)(2,1)} %copy.48), calls=%async_computation.1 | async-start | bytes 1048576 | tf_op jit(solution)/shard_map/all_to_all | solution.py:155
where the time goes:
time: 111 us; the launch traced here: 110 us
  matrix products  74.5 us (67%)
  waiting for transfers between devices  13.7 us (12%)
  starting transfers between devices  13.3 us (12%)
  local copies, waits for them, and re-layouts  5.02 us (5%)
  other arithmetic  3.51 us (3%)
    all_to_all x1, waiting for transfers between devices, per_device(): lax.all_to_all(local_conv.reshape(own, length).astype(jnp.bfloat16), 'seq...  13.7 us
    dot_general x2, matrix products, spectrum_of(): jnp.einsum('rdb,rob->rod', cosines, part_imag, preferred_element_type=jnp...  11.7 us
    dot_general x2, matrix products, spectrum_of(): jnp.einsum('rdb,rob->rod', cosines, part_real, preferred_element_type=jnp...  11.5 us
    dot_general x2, matrix products, spectrum_of(): jnp.einsum('rdb,rob->rod', sines, part_imag, preferred_element_type=jnp.f...  10.9 us
    dot_general x2, matrix products, spectrum_of(): jnp.einsum('rdb,rob->rod', sines, part_real, preferred_element_type=jnp.f...  10.3 us
    all_to_all x1, starting transfers between devices, per_device(): lax.all_to_all(gated.T, 'seq', split_axis=0, concat_axis=1, tiled=True)  7.28 us
    all_to_all x1, starting transfers between devices, per_device(): lax.all_to_all(local_conv.reshape(own, length).astype(jnp.bfloat16), 'seq...  5.98 us
    dot_general x1, matrix products, row_group(): jnp.einsum('rdb,rod->rob', cosines, prod_imag, preferred_element_type=jnp...  5.75 us
  transfers between devices with their start and end apart: 2, of which 1 were waited for; matrix products, arithmetic and copies ran while one was open for 27% of the time, Pallas kernels for 0%

commit v1 on v0

--- a/solution.py
+++ b/solution.py
@@ -1,12 +1,414 @@
+import functools
+import math
+
 import jax
 import jax.numpy as jnp
+import ml_dtypes
+import numpy as np
 from jax import lax
+from jax.experimental import pallas as pl
+from jax.experimental.pallas import tpu as pltpu
 from jax.sharding import PartitionSpec as P
 
 TWO_PI = 6.283185307179586
 FLOOR_SHIFT = 0.05
 EPSILON = 1e-06
 HIGHEST = lax.Precision.HIGHEST
+LANES = 128
+MIB = 1024 * 1024
+
+
+def row_matrices(blocks, span):
+    rows_freq = 2 * blocks
+    period = rows_freq * span
+    ids = np.arange(span, dtype=np.int64)
+    wave = np.arange(blocks + 1)[:, None] + rows_freq * ids[None, :]
+    turns = (wave[:, :, None] * ids[None, None, :]) % period
+    angle = turns.astype(np.float32) * np.float32(TWO_PI / period)
+    cosines, sines = np.cos(angle), np.sin(angle)
+    upper = np.concatenate([cosines, sines], axis=2)
+    lower = np.concatenate([-sines, cosines], axis=2)
+    forward = np.concatenate([upper, lower], axis=1).astype(ml_dtypes.bfloat16)
+    return forward, np.ascontiguousarray(forward.transpose(0, 2, 1))
+
+
+def position_features(length, emb):
+    band_count = (emb - 1) // 2
+    position_f = np.arange(length, dtype=np.float32)
+    moments = position_f / np.float32(length - 1)
+    phases = position_f * np.float32(TWO_PI / length)
+    tones = np.linspace(0.0001, band_count - 1, band_count).astype(np.float32)
+    angles = tones[:, None] * phases[None, :]
+    return np.concatenate([moments[None, :], np.cos(angles), -np.sin(angles)], axis=0)
+
+
+def sine(value):
+    turns = jnp.round(value * (1.0 / math.pi))
+    rest = value - turns * 3.140625
+    rest = rest - turns * 9.67502593994140625e-4
+    rest = rest - turns * 1.509957990978376432e-7
+    parity = turns - 2.0 * jnp.floor(turns * 0.5)
+    square = rest * rest
+    poly = -2.3889859e-08 * square + 2.7525562e-06
+    poly = poly * square - 0.00019840874
+    poly = poly * square + 0.0083333310
+    poly = poly * square - 0.16666667
+    signed = rest - 2.0 * parity * rest
+    return signed + signed * (square * poly)
+
+
+def weighted(terms):
+    total = None
+    for factor, value in terms:
+        if abs(factor) < 1e-9:
+            continue
+        if abs(factor - 1.0) < 1e-9:
+            total = value if total is None else total + value
+        elif abs(factor + 1.0) < 1e-9:
+            total = -value if total is None else total - value
+        else:
+            part = value * factor
+            total = part if total is None else total + part
+    return total
+
+
+def sections(load, store, blocks):
+    half = blocks // 2
+    x = [load(a).astype(jnp.float32) for a in range(blocks)]
+    plus = {a: x[a] + x[blocks - a] for a in range(1, half)}
+    minus = {a: x[a] - x[blocks - a] for a in range(1, half)}
+    for c in range(blocks + 1):
+        step = math.pi * c / blocks
+        even = c % 2 == 0
+        on_cos, on_sin = (plus, minus) if even else (minus, plus)
+        middle = [(math.cos(step * half), x[half])] if even else []
+        real = weighted([(1.0, x[0])] + middle + [(math.cos(step * a), on_cos[a]) for a in on_cos])
+        store(c, 0, real.astype(jnp.bfloat16))
+        if 0 < c < blocks:
+            middle = [] if even else [(-math.sin(step * half), x[half])]
+            imag = weighted(middle + [(-math.sin(step * a), on_sin[a]) for a in on_sin])
+            store(c, 1, imag.astype(jnp.bfloat16))
+
+
+def joined(load, store, blocks, factor):
+    half = blocks // 2
+    real = [load(c, 0) * (factor if c in (0, blocks) else 2.0 * factor) for c in range(blocks + 1)]
+    imag = {c: load(c, 1) * (2.0 * factor) for c in range(1, blocks)}
+    for a in range(half + 1):
+        step = math.pi * a / blocks
+        even_cos = weighted([(math.cos(step * c), real[c]) for c in range(0, blocks + 1, 2)])
+        odd_cos = weighted([(math.cos(step * c), real[c]) for c in range(1, blocks + 1, 2)])
+        even_sin = weighted([(math.sin(step * c), imag[c]) for c in range(2, blocks, 2)])
+        odd_sin = weighted([(math.sin(step * c), imag[c]) for c in range(1, blocks, 2)])
+        both = even_cos if odd_sin is None else even_cos - odd_sin
+        turn = None
+        if odd_cos is not None and even_sin is not None:
+            turn = odd_cos - even_sin
+        elif odd_cos is not None:
+            turn = odd_cos
+        elif even_sin is not None:
+            turn = -even_sin
+        store(a, (both if turn is None else both + turn).astype(jnp.bfloat16))
+        if 0 < a < half:
+            store(blocks - a, (both if turn is None else both - turn).astype(jnp.bfloat16))
+
+
+def partner(me, mask, count):
+    total, bit = 0, 1
+    while bit < count:
+        digit = (me // bit) % 2
+        total = total + bit * ((1 - digit) if mask & bit else digit)
+        bit *= 2
+    return total
+
+
+def layer_kernel(
+    blocks,
+    span,
+    own,
+    signal,
+    gate_in,
+    gate_out,
+    features,
+    pos_weight,
+    pos_bias,
+    inner_weight,
+    inner_bias,
+    frequency,
+    out_weight,
+    decay_rates,
+    skip_gain,
+    forward_hbm,
+    inverse_hbm,
+    out,
+    forward,
+    inverse,
+    gated,
+    inbox,
+    outbox,
+    returned,
+    hidden,
+    taps,
+    tap_rows,
+    filt,
+    data_rows,
+    back,
+    table_sem,
+    send_sem,
+    recv_sem,
+):
+    me = lax.axis_index("seq")
+    chunks = own // LANES
+    length = blocks * span
+    masks = list(range(blocks - 1, 0, -1))
+    peers = {mask: partner(me, mask, blocks) for mask in masks}
+
+    barrier = pltpu.get_barrier_semaphore()
+    for mask in masks:
+        pl.semaphore_signal(
+            barrier, inc=1, device_id={"seq": peers[mask]}, device_id_type=pl.DeviceIdType.MESH
+        )
+    tables = [
+        pltpu.make_async_copy(forward_hbm, forward, table_sem.at[0]),
+        pltpu.make_async_copy(inverse_hbm, inverse, table_sem.at[1]),
+    ]
+    for copy in tables:
+        copy.start()
+
+    for chunk in range(chunks):
+        for owner in range(blocks):
+            columns = pl.ds(owner * own + chunk * LANES, LANES)
+            gated[owner, chunk] = (
+                gate_in[0, :, columns].astype(jnp.float32)
+                * signal[0, :, columns].astype(jnp.float32)
+            ).astype(jnp.bfloat16)
+    pl.semaphore_wait(barrier, len(masks))
+
+    def exchange(phase, chunk, source_of, target):
+        copies = []
+        for mask in masks:
+            copy = pltpu.make_async_remote_copy(
+                src_ref=source_of(peers[mask]),
+                dst_ref=target.at[chunk, me],
+                send_sem=send_sem.at[phase, chunk, mask],
+                recv_sem=recv_sem.at[phase, chunk, mask],
+                device_id={"seq": peers[mask]},
+                device_id_type=pl.DeviceIdType.MESH,
+            )
+            copy.start()
+            copies.append(copy)
+        return copies
+
+    incoming = [
+        exchange(0, chunk, lambda peer, chunk=chunk: gated.at[peer, chunk], inbox)
+        for chunk in range(chunks)
+    ]
+    for chunk in range(chunks):
+        inbox[chunk, me] = gated[me, chunk]
+
+    order = frequency.shape[1]
+    diagonal = lax.broadcasted_iota(jnp.int32, (order, order), 0) == lax.broadcasted_iota(
+        jnp.int32, (order, order), 1
+    )
+
+    def as_column(row):
+        return jnp.sum(jnp.where(diagonal, row, 0.0), axis=1, keepdims=True)
+
+    def layer(weight, values, bias):
+        product = lax.dot_general(
+            weight,
+            values,
+            (((0,), (0,)), ((), ())),
+            precision=HIGHEST,
+            preferred_element_type=jnp.float32,
+        )
+        return sine(rate * (product + as_column(bias)))
+
+    rate = as_column(frequency[...])
+    hidden[...] = layer(pos_weight[...], features[...], pos_bias[...])
+    for index in range(inner_weight.shape[0]):
+        hidden[...] = layer(inner_weight[index], hidden[...], inner_bias[pl.ds(index, 1), :])
+    mine = pl.ds(pl.multiple_of(me * own, LANES), own)
+    weight = out_weight[:, mine]
+    decay = decay_rates[:, mine]
+    energy = jnp.zeros((1, own), jnp.float32)
+    for a in range(blocks):
+        place = lax.broadcasted_iota(jnp.int32, (span, own), 0) + a * span
+        moment = place.astype(jnp.float32) / float(length - 1)
+        raw = lax.dot_general(
+            hidden[:, a * span : (a + 1) * span],
+            weight,
+            (((0,), (0,)), ((), ())),
+            precision=HIGHEST,
+            preferred_element_type=jnp.float32,
+        ) * (jnp.exp(-moment * decay) + FLOOR_SHIFT)
+        energy = energy + jnp.sum(raw * raw, axis=0, keepdims=True)
+        taps[a] = raw.astype(jnp.bfloat16)
+    scale = lax.rsqrt(energy + EPSILON)
+
+    group = 16
+
+    def tap_section(step, carry):
+        rows = pl.ds(pl.multiple_of(step * group, group), group)
+
+        def store(c, part, value):
+            tap_rows[c, part, rows, :] = value
+
+        sections(lambda a: taps[a, rows, :], store, blocks)
+        return carry
+
+    lax.fori_loop(0, span // group, tap_section, 0)
+    for copy in tables:
+        copy.wait()
+
+    def spectrum(c, rows):
+        if c in (0, blocks):
+            table, data = forward[c, :, :span], rows[0]
+        else:
+            table, data = forward[c], jnp.concatenate([rows[0], rows[1]], axis=0)
+        return jnp.dot(table, data, preferred_element_type=jnp.float32)
+
+    for c in range(blocks + 1):
+        filt[c] = spectrum(c, tap_rows.at[c]) * scale
+
+    outgoing = []
+    for chunk in range(chunks):
+        for copy in incoming[chunk]:
+            copy.wait_recv()
+
+        def data_section(step, carry):
+            rows = pl.ds(pl.multiple_of(step * group, group), group)
+
+            def store(c, part, value):
+                data_rows[c, part, rows, :] = value
+
+            sections(lambda a: inbox[chunk, a, rows, :], store, blocks)
+            return carry
+
+        lax.fori_loop(0, span // group, data_section, 0)
+        lanes = slice(chunk * LANES, (chunk + 1) * LANES)
+        for c in range(blocks + 1):
+            wave = spectrum(c, data_rows.at[c])
+            wave_real, wave_imag = wave[:span], wave[span:]
+            filt_real, filt_imag = filt[c, :span, lanes], filt[c, span:, lanes]
+            product = jnp.concatenate(
+                [
+                    (wave_real * filt_real - wave_imag * filt_imag).astype(jnp.bfloat16),
+                    (wave_real * filt_imag + wave_imag * filt_real).astype(jnp.bfloat16),
+                ],
+                axis=0,
+            )
+            if c in (0, blocks):
+                back[c, :span] = jnp.dot(
+                    inverse[c, :span, :], product, preferred_element_type=jnp.float32
+                )
+            else:
+                back[c] = jnp.dot(inverse[c], product, preferred_element_type=jnp.float32)
+
+        def join_section(step, carry):
+            small = 8
+
+            def load(c, part):
+                return back[c, pl.ds(pl.multiple_of(part * span + step * group, small), group), :]
+
+            def store(a, value):
+                outbox[chunk, a, pl.ds(pl.multiple_of(step * group, group), group), :] = value
+
+            joined(load, store, blocks, 1.0 / (2 * length))
+            return carry
+
+        lax.fori_loop(0, span // group, join_section, 0)
+        outgoing.append(
+            exchange(1, chunk, lambda peer, chunk=chunk: outbox.at[chunk, peer], returned)
+        )
+
+    def finish(chunk, owner, convolved):
+        columns = pl.ds(pl.multiple_of(owner * own + chunk * LANES, LANES), LANES)
+        out[0, :, columns] = (
+            gate_out[0, :, columns].astype(jnp.float32)
+            * (
+                convolved.astype(jnp.float32)
+                + skip_gain[:, columns] * gated[owner, chunk].astype(jnp.float32)
+            )
+        ).astype(jnp.bfloat16)
+
+    for chunk in range(chunks):
+        finish(chunk, me, outbox[chunk, me])
+    for chunk in range(chunks):
+        for mask, copy in reversed(list(zip(masks, outgoing[chunk]))):
+            copy.wait_recv()
+            finish(chunk, peers[mask], returned[chunk, peers[mask]])
+    for copies in incoming + outgoing:
+        for copy in copies:
+            copy.wait_send()
+
+
+def fused(
+    signal,
+    gate_in,
+    gate_out,
+    pos_weight,
+    pos_bias,
+    inner_weight,
+    inner_bias,
+    frequency,
+    out_weight,
+    decay_rates,
+    skip_gain,
+):
+    blocks = lax.axis_size("seq")
+    span, width = signal.shape[1], signal.shape[2]
+    own = width // blocks
+    chunks = own // LANES
+    length = span * blocks
+    order = frequency.shape[0]
+    forward, inverse = row_matrices(blocks, span)
+    features = position_features(length, pos_weight.shape[0])
+    vmem = pl.BlockSpec(memory_space=pltpu.VMEM)
+    anywhere = pl.BlockSpec(memory_space=pl.ANY)
+    bf16, f32 = jnp.bfloat16, jnp.float32
+    return pl.pallas_call(
+        functools.partial(layer_kernel, blocks, span, own),
+        out_shape=jax.ShapeDtypeStruct(signal.shape, bf16),
+        in_specs=[vmem] * 12 + [anywhere] * 2,
+        out_specs=vmem,
+        scratch_shapes=[
+            pltpu.VMEM(forward.shape, bf16),
+            pltpu.VMEM(inverse.shape, bf16),
+            pltpu.VMEM((blocks, chunks, span, LANES), bf16),
+            pltpu.VMEM((chunks, blocks, span, LANES), bf16),
+            pltpu.VMEM((chunks, blocks, span, LANES), bf16),
+            pltpu.VMEM((chunks, blocks, span, LANES), bf16),
+            pltpu.VMEM((order, length), f32),
+            pltpu.VMEM((blocks, span, own), bf16),
+            pltpu.VMEM((blocks + 1, 2, span, own), bf16),
+            pltpu.VMEM((blocks + 1, 2 * span, own), f32),
+            pltpu.VMEM((blocks + 1, 2, span, LANES), bf16),
+            pltpu.VMEM((blocks + 1, 2 * span, LANES), f32),
+            pltpu.SemaphoreType.DMA((2,)),
+            pltpu.SemaphoreType.DMA((2, chunks, blocks)),
+            pltpu.SemaphoreType.DMA((2, chunks, blocks)),
+        ],
+        compiler_params=pltpu.CompilerParams(
+            collective_id=0, has_side_effects=True, vmem_limit_bytes=40 * MIB
+        ),
+        name="hyena_layer",
+    )(
+        signal,
+        gate_in,
+        gate_out,
+        jnp.asarray(features),
+        pos_weight,
+        pos_bias.reshape(1, -1),
+        inner_weight,
+        inner_bias,
+        frequency.reshape(1, -1),
+        out_weight,
+        decay_rates.reshape(1, -1),
+        skip_gain.reshape(1, -1),
+        jnp.asarray(forward),
+        jnp.asarray(inverse),
+    )
 
 
 def unit_angle(index, period):
@@ -41,7 +443,7 @@
     return (hidden, moments)
 
 
-def per_device(
+def plain(
     signal,
     gate_in,
     gate_out,
@@ -166,6 +568,18 @@
     return mixed.astype(jnp.bfloat16)[None]
 
 
+def fits_kernel(blocks, span, width):
+    own = width // blocks
+    power = blocks >= 4 and blocks & (blocks - 1) == 0
+    return power and span == LANES and own > 0 and own % LANES == 0
+
+
+def per_device(signal, *rest):
+    if fits_kernel(lax.axis_size("seq"), signal.shape[1], signal.shape[2]):
+        return fused(signal, *rest)
+    return plain(signal, *rest)
+
+
 def solution(mesh):
     return jax.shard_map(
         per_device,

time: 111 us -> 44.2 us (0.40)
  matrix products: 74.5 us -> 0 us
  Pallas kernels: 0 us -> 30.2 us
  waiting for transfers between devices: 13.7 us -> 0 us
  starting transfers between devices: 13.3 us -> 0 us
  local copies, waits for them, and re-layouts: 5.02 us -> 13.4 us
  other arithmetic: 3.51 us -> 0 us
    dot_general x22 -> x0, matrix products: 74.5 us -> none  [the longest x2 11.7 us: spectrum_of(): jnp.einsum('rdb,rob->rod', cosines, part_imag, preferred_element_type=jnp...]
    pallas_call x0 -> x1, Pallas kernels: none -> 30.2 us  [fused(): pl.pallas_call(functools.partial(layer_kernel, blocks, span, own), out_sh...]
    all_to_all x2 -> x0, waiting for transfers between devices: 13.7 us -> none  [the longest x1 13.7 us: per_device(): lax.all_to_all(local_conv.reshape(own, length).astype(jnp.bfloat16), 'seq...]
    all_to_all x2 -> x0, starting transfers between devices: 13.3 us -> none  [the longest x1 7.28 us: per_device(): lax.all_to_all(gated.T, 'seq', split_axis=0, concat_axis=1, tiled=True)]
    unnamed x20 -> x29, local copies, waits for them, and re-layouts: 3.12 us -> 13.4 us
    convert_element_type x2 -> x0, other arithmetic: 2.31 us -> none  [the longest x1 1.38 us: per_device(): return mixed.astype(jnp.bfloat16)[None]]
  transfers between devices with their start and end apart: 2 -> 0, of which waited for: 1 -> 0; matrix products, arithmetic and copies ran while one was open for 27% -> 0% of each run, Pallas kernels for 0% -> 0%
where the time goes in v1:
time: 44.2 us; the launch traced here: 43.6 us
  Pallas kernels  30.2 us (68%)
  local copies, waits for them, and re-layouts  13.4 us (30%)
    pallas_call x1, Pallas kernels, fused(): pl.pallas_call(functools.partial(layer_kernel, blocks, span, own), out_sh...  30.2 us
    unnamed x29, local copies, waits for them, and re-layouts  13.4 us

profile of v1, /device:TPU:0, one launch (start us, length us, event | category | flops | bytes accessed | tf_op | source)
XLA Modules:
  0.0 43.6 jit_solution(2622941149573043778)
XLA Ops:
  0.0 0.0 copy-start
  0.0 1.3 %copy-done = bf16[9,256,256]{2,1,0:T(8,128)(2,1)S(1)} copy-done((bf16[9,256,256]{2,1,0:T(8,128)(2,1)S(1)}, bf16[9,256,256]{2,1,0:T(8,128)(2,1)}, u32[]{:S(2)}) %copy-start) | copy-done | bytes 1179672
  1.3 0.0 copy-start.1
  1.3 1.3 %copy-done.1 = bf16[9,256,256]{2,1,0:T(8,128)(2,1)S(1)} copy-done((bf16[9,256,256]{2,1,0:T(8,128)(2,1)S(1)}, bf16[9,256,256]{2,1,0:T(8,128)(2,1)}, u32[]{:S(2)}) %copy-start.1) | copy-done | bytes 1179672
  2.5 0.0 copy-start.2
  2.5 1.0 %copy-done.2 = bf16[1,128,2048]{2,1,0:T(8,128)(2,1)S(1)} copy-done((bf16[1,128,2048]{2,1,0:T(8,128)(2,1)S(1)}, bf16[1,128,2048]{2,1,0:T(8,128)(2,1)}, u32[]{:S(2)}) %copy-start.2) | copy-done | bytes 524312
  3.6 0.0 copy-start.3
  3.6 1.0 %copy-done.3 = bf16[1,128,2048]{2,1,0:T(8,128)(2,1)S(1)} copy-done((bf16[1,128,2048]{2,1,0:T(8,128)(2,1)S(1)}, bf16[1,128,2048]{2,1,0:T(8,128)(2,1)}, u32[]{:S(2)}) %copy-start.3) | copy-done | bytes 524312
  4.6 0.0 copy-start.4
  4.6 1.0 %copy-done.4 = bf16[1,128,2048]{2,1,0:T(8,128)(2,1)S(1)} copy-done((bf16[1,128,2048]{2,1,0:T(8,128)(2,1)S(1)}, bf16[1,128,2048]{2,1,0:T(8,128)(2,1)}, u32[]{:S(2)}) %copy-start.4) | copy-done | bytes 524312
  5.7 0.0 copy-start.5
  5.7 1.0 %copy-done.5 = f32[64,2048]{1,0:T(8,128)S(1)} copy-done((f32[64,2048]{1,0:T(8,128)S(1)}, f32[64,2048]{1,0:T(8,128)}, u32[]{:S(2)}) %copy-start.5) | copy-done | bytes 524312
  6.7 0.0 copy-start.6
  6.7 0.9 %copy-done.6 = f32[33,1024]{1,0:T(8,128)S(1)} copy-done((f32[33,1024]{1,0:T(8,128)S(1)}, f32[33,1024]{1,0:T(8,128)}, u32[]{:S(2)}) %copy-start.6) | copy-done | bytes 135192
  7.6 0.0 copy-start.7
  7.6 0.8 %copy-done.7 = f32[2,64,64]{2,1,0:T(8,128)S(1)} copy-done((f32[2,64,64]{2,1,0:T(8,128)S(1)}, f32[2,64,64]{2,1,0:T(8,128)}, u32[]{:S(2)}) %copy-start.7) | copy-done | bytes 32792
  8.5 0.0 copy-start.8
  8.5 0.7 %copy-done.8 = f32[33,64]{1,0:T(8,128)S(1)} copy-done((f32[33,64]{1,0:T(8,128)S(1)}, f32[33,64]{1,0:T(8,128)}, u32[]{:S(2)}) %copy-start.8) | copy-done | bytes 8472
  9.2 0.0 copy-start.9
  9.2 0.7 %copy-done.9 = f32[2048]{0:T(1024)S(1)} copy-done((f32[2048]{0:T(1024)S(1)}, f32[2048]{0:T(1024)}, u32[]{:S(2)}) %copy-start.9) | copy-done | bytes 8216
  9.9 0.0 copy-start.10
  9.9 0.7 %copy-done.10 = f32[2048]{0:T(1024)S(1)} copy-done((f32[2048]{0:T(1024)S(1)}, f32[2048]{0:T(1024)}, u32[]{:S(2)}) %copy-start.10) | copy-done | bytes 8216
  10.6 0.0 copy-start.11
  10.6 0.7 %copy-done.11 = f32[2,64]{1,0:T(2,128)S(1)} copy-done((f32[2,64]{1,0:T(2,128)S(1)}, f32[2,64]{1,0:T(2,128)}, u32[]{:S(2)}) %copy-start.11) | copy-done | bytes 536
  11.3 0.0 copy-start.12
  11.3 0.7 %copy-done.12 = f32[64]{0:T(128)S(1)} copy-done((f32[64]{0:T(128)S(1)}, f32[64]{0:T(128)}, u32[]{:S(2)}) %copy-start.12) | copy-done | bytes 280
  11.9 0.0 copy-start.13
  11.9 0.7 %copy-done.13 = f32[64]{0:T(128)S(1)} copy-done((f32[64]{0:T(128)S(1)}, f32[64]{0:T(128)}, u32[]{:S(2)}) %copy-start.13) | copy-done | bytes 280
  12.6 30.2 %hyena_layer.1 = bf16[1,128,2048]{2,1,0:T(8,128)(2,1)S(1)} custom-call(bf16[1,128,2048]{2,1,0:T(8,128)(2,1)S(1)} %copy-done.2, bf16[1,128,2048]{2,1,0:T(8,128)(2,1)S(1)} %copy-done.3, bf16[1,128,2048]{2,1,0:T(8,128)(2,1)S(1)} %copy-done.4, f32[33,1024]{1,0:T(8,128)S(1)} %copy-done.6, f32[33,64]{1,0:T(8,128)S(1)} %copy-done.8, f32[1,64]{1,0:T(1,128)S(1)} %bitcast.6, ...), custom_call_target="tpu_custom_call" | custom-call | tf_op jit(solution)/shard_map/hyena_layer/pallas_call | solution.py:370
  42.8 0.8 %copy.16 = bf16[1,128,2048]{2,1,0:T(8,128)(2,1)} copy(bf16[1,128,2048]{2,1,0:T(8,128)(2,1)S(1)} %hyena_layer.1) | data formatting | bytes 1048576
Async XLA Ops:
  0.0 1.3 %copy-start = (bf16[9,256,256]{2,1,0:T(8,128)(2,1)S(1)}, bf16[9,256,256]{2,1,0:T(8,128)(2,1)}, u32[]{:S(2)}) copy-start(bf16[9,256,256]{2,1,0:T(8,128)(2,1)} %constant.8.clone.inverse_hbm) | copy-start | bytes 3538948
  1.3 1.3 %copy-start.1 = (bf16[9,256,256]{2,1,0:T(8,128)(2,1)S(1)}, bf16[9,256,256]{2,1,0:T(8,128)(2,1)}, u32[]{:S(2)}) copy-start(bf16[9,256,256]{2,1,0:T(8,128)(2,1)} %constant.7.clone.forward_hbm) | copy-start | bytes 3538948
  2.5 1.0 %copy-start.2 = (bf16[1,128,2048]{2,1,0:T(8,128)(2,1)S(1)}, bf16[1,128,2048]{2,1,0:T(8,128)(2,1)}, u32[]{:S(2)}) copy-start(bf16[1,128,2048]{2,1,0:T(8,128)(2,1)} %signal.1) | copy-start | bytes 1572868
  3.6 1.0 %copy-start.3 = (bf16[1,128,2048]{2,1,0:T(8,128)(2,1)S(1)}, bf16[1,128,2048]{2,1,0:T(8,128)(2,1)}, u32[]{:S(2)}) copy-start(bf16[1,128,2048]{2,1,0:T(8,128)(2,1)} %gate_in.1) | copy-start | bytes 1572868
  4.6 1.0 %copy-start.4 = (bf16[1,128,2048]{2,1,0:T(8,128)(2,1)S(1)}, bf16[1,128,2048]{2,1,0:T(8,128)(2,1)}, u32[]{:S(2)}) copy-start(bf16[1,128,2048]{2,1,0:T(8,128)(2,1)} %gate_out.1) | copy-start | bytes 1572868
  5.7 1.0 %copy-start.5 = (f32[64,2048]{1,0:T(8,128)S(1)}, f32[64,2048]{1,0:T(8,128)}, u32[]{:S(2)}) copy-start(f32[64,2048]{1,0:T(8,128)} %out_weight.1) | copy-start | bytes 1572868
  6.7 0.9 %copy-start.6 = (f32[33,1024]{1,0:T(8,128)S(1)}, f32[33,1024]{1,0:T(8,128)}, u32[]{:S(2)}) copy-start(f32[33,1024]{1,0:T(8,128)} %constant.6.clone.features) | copy-start | bytes 405508
  7.6 0.8 %copy-start.7 = (f32[2,64,64]{2,1,0:T(8,128)S(1)}, f32[2,64,64]{2,1,0:T(8,128)}, u32[]{:S(2)}) copy-start(f32[2,64,64]{2,1,0:T(8,128)} %inner_weight.1) | copy-start | bytes 98308
  8.5 0.7 %copy-start.8 = (f32[33,64]{1,0:T(8,128)S(1)}, f32[33,64]{1,0:T(8,128)}, u32[]{:S(2)}) copy-start(f32[33,64]{1,0:T(8,128)} %pos_weight.1) | copy-start | bytes 25348
  9.2 0.7 %copy-start.9 = (f32[2048]{0:T(1024)S(1)}, f32[2048]{0:T(1024)}, u32[]{:S(2)}) copy-start(f32[2048]{0:T(1024)} %param.23) | copy-start | bytes 24580
  9.9 0.7 %copy-start.10 = (f32[2048]{0:T(1024)S(1)}, f32[2048]{0:T(1024)}, u32[]{:S(2)}) copy-start(f32[2048]{0:T(1024)} %param.24) | copy-start | bytes 24580
  10.6 0.7 %copy-start.11 = (f32[2,64]{1,0:T(2,128)S(1)}, f32[2,64]{1,0:T(2,128)}, u32[]{:S(2)}) copy-start(f32[2,64]{1,0:T(2,128)} %inner_bias.1) | copy-start | bytes 1540
  11.3 0.7 %copy-start.12 = (f32[64]{0:T(128)S(1)}, f32[64]{0:T(128)}, u32[]{:S(2)}) copy-start(f32[64]{0:T(128)} %param.18) | copy-start | bytes 772
  11.9 0.7 %copy-start.13 = (f32[64]{0:T(128)S(1)}, f32[64]{0:T(128)}, u32[]{:S(2)}) copy-start(f32[64]{0:T(128)} %param.21) | copy-start | bytes 772

commit v2 on v1

--- a/solution.py
+++ b/solution.py
@@ -126,6 +126,21 @@
     blocks,
     span,
     own,
+    signal_hbm,
+    gate_in_hbm,
+    gate_out_hbm,
+    features_hbm,
+    pos_weight_hbm,
+    pos_bias_hbm,
+    inner_weight_hbm,
+    inner_bias_hbm,
+    frequency_hbm,
+    out_weight_hbm,
+    decay_rates_hbm,
+    skip_gain_hbm,
+    forward_hbm,
+    inverse_hbm,
+    out,
     signal,
     gate_in,
     gate_out,
@@ -135,12 +150,9 @@
     inner_weight,
     inner_bias,
     frequency,
-    out_weight,
-    decay_rates,
+    weight,
+    decay,
     skip_gain,
-    forward_hbm,
-    inverse_hbm,
-    out,
     forward,
     inverse,
     gated,
@@ -153,7 +165,7 @@
     filt,
     data_rows,
     back,
-    table_sem,
+    load_sem,
     send_sem,
     recv_sem,
 ):
@@ -168,13 +180,32 @@
         pl.semaphore_signal(
             barrier, inc=1, device_id={"seq": peers[mask]}, device_id_type=pl.DeviceIdType.MESH
         )
-    tables = [
-        pltpu.make_async_copy(forward_hbm, forward, table_sem.at[0]),
-        pltpu.make_async_copy(inverse_hbm, inverse, table_sem.at[1]),
+    mine = pl.ds(pl.multiple_of(me * own, LANES), own)
+    pairs = [
+        (signal_hbm, signal),
+        (gate_in_hbm, gate_in),
+        (features_hbm, features),
+        (pos_weight_hbm, pos_weight),
+        (pos_bias_hbm, pos_bias),
+        (frequency_hbm, frequency),
+        (inner_weight_hbm, inner_weight),
+        (inner_bias_hbm, inner_bias),
+        (out_weight_hbm.at[:, mine], weight),
+        (decay_rates_hbm.at[:, mine], decay),
+        (forward_hbm, forward),
+        (inverse_hbm, inverse),
+        (gate_out_hbm, gate_out),
+        (skip_gain_hbm, skip_gain),
     ]
-    for copy in tables:
+    loads = [
+        pltpu.make_async_copy(source, target, load_sem.at[index])
+        for index, (source, target) in enumerate(pairs)
+    ]
+    for copy in loads:
         copy.start()
 
+    for copy in loads[:2]:
+        copy.wait()
     for chunk in range(chunks):
         for owner in range(blocks):
             columns = pl.ds(owner * own + chunk * LANES, LANES)
@@ -224,24 +255,23 @@
         )
         return sine(rate * (product + as_column(bias)))
 
+    for copy in loads[2:10]:
+        copy.wait()
     rate = as_column(frequency[...])
     hidden[...] = layer(pos_weight[...], features[...], pos_bias[...])
     for index in range(inner_weight.shape[0]):
         hidden[...] = layer(inner_weight[index], hidden[...], inner_bias[pl.ds(index, 1), :])
-    mine = pl.ds(pl.multiple_of(me * own, LANES), own)
-    weight = out_weight[:, mine]
-    decay = decay_rates[:, mine]
     energy = jnp.zeros((1, own), jnp.float32)
     for a in range(blocks):
         place = lax.broadcasted_iota(jnp.int32, (span, own), 0) + a * span
         moment = place.astype(jnp.float32) / float(length - 1)
         raw = lax.dot_general(
             hidden[:, a * span : (a + 1) * span],
-            weight,
+            weight[...],
             (((0,), (0,)), ((), ())),
             precision=HIGHEST,
             preferred_element_type=jnp.float32,
-        ) * (jnp.exp(-moment * decay) + FLOOR_SHIFT)
+        ) * (jnp.exp(-moment * decay[...]) + FLOOR_SHIFT)
         energy = energy + jnp.sum(raw * raw, axis=0, keepdims=True)
         taps[a] = raw.astype(jnp.bfloat16)
     scale = lax.rsqrt(energy + EPSILON)
@@ -258,7 +288,7 @@
         return carry
 
     lax.fori_loop(0, span // group, tap_section, 0)
-    for copy in tables:
+    for copy in loads[10:12]:
         copy.wait()
 
     def spectrum(c, rows):
@@ -332,6 +362,8 @@
             )
         ).astype(jnp.bfloat16)
 
+    for copy in loads[12:]:
+        copy.wait()
     for chunk in range(chunks):
         finish(chunk, me, outbox[chunk, me])
     for chunk in range(chunks):
@@ -364,36 +396,9 @@
     order = frequency.shape[0]
     forward, inverse = row_matrices(blocks, span)
     features = position_features(length, pos_weight.shape[0])
-    vmem = pl.BlockSpec(memory_space=pltpu.VMEM)
-    anywhere = pl.BlockSpec(memory_space=pl.ANY)
+    hbm = pl.BlockSpec(memory_space=pltpu.HBM)
     bf16, f32 = jnp.bfloat16, jnp.float32
-    return pl.pallas_call(
-        functools.partial(layer_kernel, blocks, span, own),
-        out_shape=jax.ShapeDtypeStruct(signal.shape, bf16),
-        in_specs=[vmem] * 12 + [anywhere] * 2,
-        out_specs=vmem,
-        scratch_shapes=[
-            pltpu.VMEM(forward.shape, bf16),
-            pltpu.VMEM(inverse.shape, bf16),
-            pltpu.VMEM((blocks, chunks, span, LANES), bf16),
-            pltpu.VMEM((chunks, blocks, span, LANES), bf16),
-            pltpu.VMEM((chunks, blocks, span, LANES), bf16),
-            pltpu.VMEM((chunks, blocks, span, LANES), bf16),
-            pltpu.VMEM((order, length), f32),
-            pltpu.VMEM((blocks, span, own), bf16),
-            pltpu.VMEM((blocks + 1, 2, span, own), bf16),
-            pltpu.VMEM((blocks + 1, 2 * span, own), f32),
-            pltpu.VMEM((blocks + 1, 2, span, LANES), bf16),
-            pltpu.VMEM((blocks + 1, 2 * span, LANES), f32),
-            pltpu.SemaphoreType.DMA((2,)),
-            pltpu.SemaphoreType.DMA((2, chunks, blocks)),
-            pltpu.SemaphoreType.DMA((2, chunks, blocks)),
-        ],
-        compiler_params=pltpu.CompilerParams(
-            collective_id=0, has_side_effects=True, vmem_limit_bytes=40 * MIB
-        ),
-        name="hyena_layer",
-    )(
+    operands = (
         signal,
         gate_in,
         gate_out,
@@ -409,6 +414,35 @@
         jnp.asarray(forward),
         jnp.asarray(inverse),
     )
+    shapes = [operand.shape for operand in operands]
+    shapes[9], shapes[10] = (order, own), (1, own)
+    locals_ = [pltpu.VMEM(shape, operand.dtype) for shape, operand in zip(shapes, operands)]
+    return pl.pallas_call(
+        functools.partial(layer_kernel, blocks, span, own),
+        out_shape=jax.ShapeDtypeStruct(signal.shape, bf16),
+        in_specs=[hbm] * len(operands),
+        out_specs=pl.BlockSpec(memory_space=pltpu.VMEM),
+        scratch_shapes=[
+            *locals_,
+            pltpu.VMEM((blocks, chunks, span, LANES), bf16),
+            pltpu.VMEM((chunks, blocks, span, LANES), bf16),
+            pltpu.VMEM((chunks, blocks, span, LANES), bf16),
+            pltpu.VMEM((chunks, blocks, span, LANES), bf16),
+            pltpu.VMEM((order, length), f32),
+            pltpu.VMEM((blocks, span, own), bf16),
+            pltpu.VMEM((blocks + 1, 2, span, own), bf16),
+            pltpu.VMEM((blocks + 1, 2 * span, own), f32),
+            pltpu.VMEM((blocks + 1, 2, span, LANES), bf16),
+            pltpu.VMEM((blocks + 1, 2 * span, LANES), f32),
+            pltpu.SemaphoreType.DMA((len(operands),)),
+            pltpu.SemaphoreType.DMA((2, chunks, blocks)),
+            pltpu.SemaphoreType.DMA((2, chunks, blocks)),
+        ],
+        compiler_params=pltpu.CompilerParams(
+            collective_id=0, has_side_effects=True, vmem_limit_bytes=62 * MIB
+        ),
+        name="hyena_layer",
+    )(*operands)
 
 
 def unit_angle(index, period):

time: 44.2 us -> 33.1 us (0.75); the launches traced: 43.6 us -> 33 us
  local copies, waits for them, and re-layouts: 13.4 us -> 1.88 us
  Pallas kernels: 30.2 us -> 31.1 us
    unnamed x29 -> x1, local copies, waits for them, and re-layouts: 13.4 us -> 1.88 us
    pallas_call x1, Pallas kernels: 30.2 us -> 31.1 us  [fused(): pl.pallas_call(functools.partial(layer_kernel, blocks, span, own), out_sh...]
where the time goes in v2:
time: 33.1 us; the launch traced here: 33 us
  Pallas kernels  31.1 us (94%)
  local copies, waits for them, and re-layouts  1.88 us (6%)
    pallas_call x1, Pallas kernels, fused(): pl.pallas_call(functools.partial(layer_kernel, blocks, span, own), out_sh...  31.1 us
    unnamed x1, local copies, waits for them, and re-layouts  1.88 us

profile of v2, /device:TPU:0, one launch (start us, length us, event | category | flops | bytes accessed | tf_op | source)
XLA Modules:
  0.0 33.0 jit_solution(5947572007874305717)
XLA Ops:
  0.0 31.1 %hyena_layer.1 = bf16[1,128,2048]{2,1,0:T(8,128)(2,1)} custom-call(bf16[1,128,2048]{2,1,0:T(8,128)(2,1)} %signal_hbm.1, bf16[1,128,2048]{2,1,0:T(8,128)(2,1)} %gate_in_hbm.1, bf16[1,128,2048]{2,1,0:T(8,128)(2,1)} %gate_out_hbm.1, f32[33,1024]{1,0:T(8,128)} %constant.6.clone.features_hbm, f32[33,64]{1,0:T(8,128)} %pos_weight_hbm.1, f32[1,64]{1,0:T(1,128)} %bitcast.6, ...), custom_call_target="tpu_custom_call" | custom-call | tf_op jit(solution)/shard_map/hyena_layer/pallas_call | solution.py:420
  31.1 1.9 %copy.16 = bf16[1,128,2048]{2,1,0:T(8,128)(2,1)} copy(bf16[1,128,2048]{2,1,0:T(8,128)(2,1)} %hyena_layer.1) | data formatting | bytes 1048576

commit v3 on v2

--- a/solution.py
+++ b/solution.py
@@ -32,6 +32,10 @@
     return forward, np.ascontiguousarray(forward.transpose(0, 2, 1))
 
 
+def padded(rows):
+    return -(-rows // 8) * 8
+
+
 def position_features(length, emb):
     band_count = (emb - 1) // 2
     position_f = np.arange(length, dtype=np.float32)
@@ -39,7 +43,14 @@
     phases = position_f * np.float32(TWO_PI / length)
     tones = np.linspace(0.0001, band_count - 1, band_count).astype(np.float32)
     angles = tones[:, None] * phases[None, :]
-    return np.concatenate([moments[None, :], np.cos(angles), -np.sin(angles)], axis=0)
+    features = np.concatenate([moments[None, :], np.cos(angles), -np.sin(angles)], axis=0)
+    rest = np.pad(features, ((0, padded(emb) - emb), (0, 0)))
+    parts = []
+    for _ in range(3):
+        parts.append(rest.astype(ml_dtypes.bfloat16).astype(np.float32))
+        rest = rest - parts[-1]
+    rows = np.concatenate([parts[index] for index in RIGHT_ORDER], axis=0)
+    return rows.astype(ml_dtypes.bfloat16)
 
 
 def sine(value):
@@ -55,6 +66,28 @@
     poly = poly * square - 0.16666667
     signed = rest - 2.0 * parity * rest
     return signed + signed * (square * poly)
+
+
+def pieces(value, count):
+    parts = []
+    for _ in range(count):
+        part = value.astype(jnp.bfloat16).astype(jnp.float32)
+        parts.append(part)
+        value = value - part
+    return parts
+
+
+LEFT_ORDER, RIGHT_ORDER = (0, 1, 0, 1, 0, 2), (0, 0, 1, 1, 2, 0)
+
+
+def stacked(parts, order):
+    return jnp.concatenate([parts[index] for index in order], axis=0).astype(jnp.bfloat16)
+
+
+def stacked_dot(left, right):
+    return lax.dot_general(
+        left, right, (((0,), (0,)), ((), ())), preferred_element_type=jnp.float32
+    )
 
 
 def weighted(terms):
@@ -155,6 +188,8 @@
     skip_gain,
     forward,
     inverse,
+    staged,
+    wide_weight,
     gated,
     inbox,
     outbox,
@@ -166,6 +201,7 @@
     data_rows,
     back,
     load_sem,
+    leave_sem,
     send_sem,
     recv_sem,
 ):
@@ -245,33 +281,27 @@
     def as_column(row):
         return jnp.sum(jnp.where(diagonal, row, 0.0), axis=1, keepdims=True)
 
-    def layer(weight, values, bias):
-        product = lax.dot_general(
-            weight,
-            values,
-            (((0,), (0,)), ((), ())),
-            precision=HIGHEST,
-            preferred_element_type=jnp.float32,
-        )
-        return sine(rate * (product + as_column(bias)))
+    def layer(left, right, bias):
+        return sine(rate * (stacked_dot(left, right) + as_column(bias)))
 
     for copy in loads[2:10]:
         copy.wait()
     rate = as_column(frequency[...])
-    hidden[...] = layer(pos_weight[...], features[...], pos_bias[...])
+    wide_weight[...] = jnp.zeros_like(wide_weight)
+    wide_weight[: pos_weight.shape[0], :] = pos_weight[...]
+    left = stacked(pieces(wide_weight[...], 3), LEFT_ORDER)
+    hidden[...] = layer(left, features[...], pos_bias[...])
     for index in range(inner_weight.shape[0]):
-        hidden[...] = layer(inner_weight[index], hidden[...], inner_bias[pl.ds(index, 1), :])
+        left = stacked(pieces(inner_weight[index], 3), LEFT_ORDER)
+        right = stacked(pieces(hidden[...], 3), RIGHT_ORDER)
+        hidden[...] = layer(left, right, inner_bias[pl.ds(index, 1), :])
+    right = stacked(pieces(weight[...], 2), (0, 0, 1, 1))
     energy = jnp.zeros((1, own), jnp.float32)
     for a in range(blocks):
         place = lax.broadcasted_iota(jnp.int32, (span, own), 0) + a * span
         moment = place.astype(jnp.float32) / float(length - 1)
-        raw = lax.dot_general(
-            hidden[:, a * span : (a + 1) * span],
-            weight[...],
-            (((0,), (0,)), ((), ())),
-            precision=HIGHEST,
-            preferred_element_type=jnp.float32,
-        ) * (jnp.exp(-moment * decay[...]) + FLOOR_SHIFT)
+        left = stacked(pieces(hidden[:, a * span : (a + 1) * span], 2), (0, 1, 0, 1))
+        raw = stacked_dot(left, right) * (jnp.exp(-moment * decay[...]) + FLOOR_SHIFT)
         energy = energy + jnp.sum(raw * raw, axis=0, keepdims=True)
         taps[a] = raw.astype(jnp.bfloat16)
     scale = lax.rsqrt(energy + EPSILON)
@@ -352,24 +382,32 @@
             exchange(1, chunk, lambda peer, chunk=chunk: outbox.at[chunk, peer], returned)
         )
 
-    def finish(chunk, owner, convolved):
+    def finish(chunk, slot, owner, convolved):
         columns = pl.ds(pl.multiple_of(owner * own + chunk * LANES, LANES), LANES)
-        out[0, :, columns] = (
+        staged[0, :, columns] = (
             gate_out[0, :, columns].astype(jnp.float32)
             * (
                 convolved.astype(jnp.float32)
                 + skip_gain[:, columns] * gated[owner, chunk].astype(jnp.float32)
             )
         ).astype(jnp.bfloat16)
-
+        copy = pltpu.make_async_copy(
+            staged.at[:, :, columns], out.at[:, :, columns], leave_sem.at[chunk, slot]
+        )
+        copy.start()
+        leaving.append(copy)
+
+    leaving = []
     for copy in loads[12:]:
         copy.wait()
     for chunk in range(chunks):
-        finish(chunk, me, outbox[chunk, me])
+        finish(chunk, 0, me, outbox[chunk, me])
     for chunk in range(chunks):
         for mask, copy in reversed(list(zip(masks, outgoing[chunk]))):
             copy.wait_recv()
-            finish(chunk, peers[mask], returned[chunk, peers[mask]])
+            finish(chunk, mask, peers[mask], returned[chunk, peers[mask]])
+    for copy in leaving:
+        copy.wait()
     for copies in incoming + outgoing:
         for copy in copies:
             copy.wait_send()
@@ -421,9 +459,11 @@
         functools.partial(layer_kernel, blocks, span, own),
         out_shape=jax.ShapeDtypeStruct(signal.shape, bf16),
         in_specs=[hbm] * len(operands),
-        out_specs=pl.BlockSpec(memory_space=pltpu.VMEM),
+        out_specs=hbm,
         scratch_shapes=[
             *locals_,
+            pltpu.VMEM(signal.shape, bf16),
+            pltpu.VMEM((padded(pos_weight.shape[0]), order), f32),
             pltpu.VMEM((blocks, chunks, span, LANES), bf16),
             pltpu.VMEM((chunks, blocks, span, LANES), bf16),
             pltpu.VMEM((chunks, blocks, span, LANES), bf16),
@@ -435,6 +475,7 @@
             pltpu.VMEM((blocks + 1, 2, span, LANES), bf16),
             pltpu.VMEM((blocks + 1, 2 * span, LANES), f32),
             pltpu.SemaphoreType.DMA((len(operands),)),
+            pltpu.SemaphoreType.DMA((chunks, blocks)),
             pltpu.SemaphoreType.DMA((2, chunks, blocks)),
             pltpu.SemaphoreType.DMA((2, chunks, blocks)),
         ],

time: 33.1 us -> 33.1 us (level)
  no operation moved by 1% of the time
where the time goes in v3:
time: 33.1 us; the launch traced here: 32.9 us
  Pallas kernels  31 us (94%)
  local copies, waits for them, and re-layouts  1.88 us (6%)
    pallas_call x1, Pallas kernels, fused(): pl.pallas_call(functools.partial(layer_kernel, blocks, span, own), out_sh...  31 us
    unnamed x1, local copies, waits for them, and re-layouts  1.88 us

profile of v3, /device:TPU:0, one launch (start us, length us, event | category | flops | bytes accessed | tf_op | source)
XLA Modules:
  0.0 32.9 jit_solution(2126602531032621924)
XLA Ops:
  0.0 31.0 %hyena_layer.1 = bf16[1,128,2048]{2,1,0:T(8,128)(2,1)} custom-call(bf16[1,128,2048]{2,1,0:T(8,128)(2,1)} %signal_hbm.1, bf16[1,128,2048]{2,1,0:T(8,128)(2,1)} %gate_in_hbm.1, bf16[1,128,2048]{2,1,0:T(8,128)(2,1)} %gate_out_hbm.1, bf16[240,1024]{1,0:T(8,128)(2,1)} %constant.6.clone.features_hbm, f32[33,64]{1,0:T(8,128)} %pos_weight_hbm.1, f32[1,64]{1,0:T(1,128)} %bitcast.6, ...), custom_call_target="tpu_custom_call" | custom-call | tf_op jit(solution)/shard_map/hyena_layer/pallas_call | solution.py:458
  31.0 1.9 %copy.16 = bf16[1,128,2048]{2,1,0:T(8,128)(2,1)} copy(bf16[1,128,2048]{2,1,0:T(8,128)(2,1)} %hyena_layer.1) | data formatting | bytes 1048576

commit v4 on v3

--- a/solution.py
+++ b/solution.py
@@ -149,8 +149,8 @@
 def partner(me, mask, count):
     total, bit = 0, 1
     while bit < count:
-        digit = (me // bit) % 2
-        total = total + bit * ((1 - digit) if mask & bit else digit)
+        digit, flip = (me // bit) % 2, (mask // bit) % 2
+        total = total + bit * (digit + flip - 2 * digit * flip)
         bit *= 2
     return total
 
@@ -208,13 +208,15 @@
     me = lax.axis_index("seq")
     chunks = own // LANES
     length = blocks * span
-    masks = list(range(blocks - 1, 0, -1))
-    peers = {mask: partner(me, mask, blocks) for mask in masks}
+    far_first = list(range(blocks - 1, 0, -1))
+    near_first = far_first[blocks // 2 :] + far_first[: blocks // 2]
+    odd = lax.axis_index("grp") % 2
+    peers = [partner(me, a + (b - a) * odd, blocks) for a, b in zip(far_first, near_first)]
 
     barrier = pltpu.get_barrier_semaphore()
-    for mask in masks:
+    for peer in peers:
         pl.semaphore_signal(
-            barrier, inc=1, device_id={"seq": peers[mask]}, device_id_type=pl.DeviceIdType.MESH
+            barrier, inc=1, device_id={"seq": peer}, device_id_type=pl.DeviceIdType.MESH
         )
     mine = pl.ds(pl.multiple_of(me * own, LANES), own)
     pairs = [
@@ -249,17 +251,17 @@
                 gate_in[0, :, columns].astype(jnp.float32)
                 * signal[0, :, columns].astype(jnp.float32)
             ).astype(jnp.bfloat16)
-    pl.semaphore_wait(barrier, len(masks))
+    pl.semaphore_wait(barrier, len(peers))
 
     def exchange(phase, chunk, source_of, target):
         copies = []
-        for mask in masks:
+        for slot, peer in enumerate(peers):
             copy = pltpu.make_async_remote_copy(
-                src_ref=source_of(peers[mask]),
+                src_ref=source_of(peer),
                 dst_ref=target.at[chunk, me],
-                send_sem=send_sem.at[phase, chunk, mask],
-                recv_sem=recv_sem.at[phase, chunk, mask],
-                device_id={"seq": peers[mask]},
+                send_sem=send_sem.at[phase, chunk, slot],
+                recv_sem=recv_sem.at[phase, chunk, slot],
+                device_id={"seq": peer},
                 device_id_type=pl.DeviceIdType.MESH,
             )
             copy.start()
@@ -403,14 +405,31 @@
     for chunk in range(chunks):
         finish(chunk, 0, me, outbox[chunk, me])
     for chunk in range(chunks):
-        for mask, copy in reversed(list(zip(masks, outgoing[chunk]))):
+        for slot, (peer, copy) in enumerate(zip(peers, outgoing[chunk])):
             copy.wait_recv()
-            finish(chunk, mask, peers[mask], returned[chunk, peers[mask]])
+            finish(chunk, slot + 1, peer, returned[chunk, peer])
     for copy in leaving:
         copy.wait()
     for copies in incoming + outgoing:
         for copy in copies:
             copy.wait_send()
+
+
+def settle_kernel(source, target, sem):
+    parts = sem.shape[0]
+    rows = source.shape[1] // parts
+    copies = [
+        pltpu.make_async_copy(
+            source.at[:, pl.ds(part * rows, rows), :],
+            target.at[:, pl.ds(part * rows, rows), :],
+            sem.at[part],
+        )
+        for part in range(parts)
+    ]
+    for copy in copies:
+        copy.start()
+    for copy in copies:
+        copy.wait()
 
 
 def fused(
@@ -455,7 +474,7 @@
     shapes = [operand.shape for operand in operands]
     shapes[9], shapes[10] = (order, own), (1, own)
     locals_ = [pltpu.VMEM(shape, operand.dtype) for shape, operand in zip(shapes, operands)]
-    return pl.pallas_call(
+    mixed = pl.pallas_call(
         functools.partial(layer_kernel, blocks, span, own),
         out_shape=jax.ShapeDtypeStruct(signal.shape, bf16),
         in_specs=[hbm] * len(operands),
@@ -484,6 +503,15 @@
         ),
         name="hyena_layer",
     )(*operands)
+    return pl.pallas_call(
+        settle_kernel,
+        out_shape=jax.ShapeDtypeStruct(mixed.shape, bf16),
+        in_specs=[hbm],
+        out_specs=hbm,
+        scratch_shapes=[pltpu.SemaphoreType.DMA((blocks,))],
+        compiler_params=pltpu.CompilerParams(vmem_limit_bytes=62 * MIB),
+        name="settle",
+    )(mixed)
 
 
 def unit_angle(index, period):

time: 33.1 us -> 48.3 us (1.46)
  Pallas kernels: 31 us -> 48.1 us
  local copies, waits for them, and re-layouts: 1.88 us -> 0 us
    pallas_call x0 -> x1, Pallas kernels: none -> 17.1 us  [fused(): pl.pallas_call(settle_kernel, out_shape=jax.ShapeDtypeStruct(mixed.shape,...]
    unnamed x1 -> x0, local copies, waits for them, and re-layouts: 1.88 us -> none
where the time goes in v4:
time: 48.3 us; the launch traced here: 48.1 us
  Pallas kernels  48.1 us (100%)
    pallas_call x1, Pallas kernels, fused(): pl.pallas_call(functools.partial(layer_kernel, blocks, span, own), out_sh...  31.1 us
    pallas_call x1, Pallas kernels, fused(): pl.pallas_call(settle_kernel, out_shape=jax.ShapeDtypeStruct(mixed.shape,...  17.1 us

profile of v4, /device:TPU:0, one launch (start us, length us, event | category | flops | bytes accessed | tf_op | source)
XLA Modules:
  0.0 48.1 jit_solution(7768044914397165132)
XLA Ops:
  0.0 31.1 %hyena_layer.1.source = bf16[1,128,2048]{2,1,0:T(8,128)(2,1)} custom-call(bf16[1,128,2048]{2,1,0:T(8,128)(2,1)} %signal_hbm.1, bf16[1,128,2048]{2,1,0:T(8,128)(2,1)} %gate_in_hbm.1, bf16[1,128,2048]{2,1,0:T(8,128)(2,1)} %gate_out_hbm.1, bf16[240,1024]{1,0:T(8,128)(2,1)} %constant.6.clone.features_hbm, f32[33,64]{1,0:T(8,128)} %pos_weight_hbm.1, ...), custom_call_target="tpu_custom_call" | custom-call | tf_op jit(solution)/shard_map/hyena_layer/pallas_call | solution.py:477
  31.1 17.1 %settle.1 = bf16[1,128,2048]{2,1,0:T(8,128)(2,1)} custom-call(bf16[1,128,2048]{2,1,0:T(8,128)(2,1)} %hyena_layer.1.source), custom_call_target="tpu_custom_call" | custom-call | tf_op jit(solution)/shard_map/settle/pallas_call | solution.py:506

commit v5 on v3

--- a/solution.py
+++ b/solution.py
@@ -242,13 +242,16 @@
 
     for copy in loads[:2]:
         copy.wait()
-    for chunk in range(chunks):
+    def gate(chunk):
         for owner in range(blocks):
             columns = pl.ds(owner * own + chunk * LANES, LANES)
             gated[owner, chunk] = (
                 gate_in[0, :, columns].astype(jnp.float32)
                 * signal[0, :, columns].astype(jnp.float32)
             ).astype(jnp.bfloat16)
+        inbox[chunk, me] = gated[me, chunk]
+
+    gate(0)
     pl.semaphore_wait(barrier, len(masks))
 
     def exchange(phase, chunk, source_of, target):
@@ -266,12 +269,12 @@
             copies.append(copy)
         return copies
 
-    incoming = [
-        exchange(0, chunk, lambda peer, chunk=chunk: gated.at[peer, chunk], inbox)
-        for chunk in range(chunks)
-    ]
-    for chunk in range(chunks):
-        inbox[chunk, me] = gated[me, chunk]
+    def depart(chunk):
+        return exchange(0, chunk, lambda peer: gated.at[peer, chunk], inbox)
+
+    incoming = [depart(0)]
+    for chunk in range(1, chunks):
+        gate(chunk)
 
     order = frequency.shape[1]
     diagonal = lax.broadcasted_iota(jnp.int32, (order, order), 0) == lax.broadcasted_iota(
@@ -306,6 +309,11 @@
         taps[a] = raw.astype(jnp.bfloat16)
     scale = lax.rsqrt(energy + EPSILON)
 
+    for chunk in range(1, chunks):
+        for copy in incoming[chunk - 1]:
+            copy.wait_send()
+        incoming.append(depart(chunk))
+
     group = 16
 
     def tap_section(step, carry):
@@ -408,7 +416,7 @@
             finish(chunk, mask, peers[mask], returned[chunk, peers[mask]])
     for copy in leaving:
         copy.wait()
-    for copies in incoming + outgoing:
+    for copies in incoming[-1:] + outgoing:
         for copy in copies:
             copy.wait_send()
 

time: 33.1 us -> 32.6 us (0.985)
  Pallas kernels: 31 us -> 30.6 us
    pallas_call x1, Pallas kernels: 31 us -> 30.6 us  [fused(): pl.pallas_call(functools.partial(layer_kernel, blocks, span, own), out_sh...]
where the time goes in v5:
time: 32.6 us; the launch traced here: 32.5 us
  Pallas kernels  30.6 us (94%)
  local copies, waits for them, and re-layouts  1.88 us (6%)
    pallas_call x1, Pallas kernels, fused(): pl.pallas_call(functools.partial(layer_kernel, blocks, span, own), out_sh...  30.6 us
    unnamed x1, local copies, waits for them, and re-layouts  1.88 us

profile of v5, /device:TPU:0, one launch (start us, length us, event | category | flops | bytes accessed | tf_op | source)
XLA Modules:
  0.0 32.5 jit_solution(970283953256037537)
XLA Ops:
  0.0 30.6 %hyena_layer.1 = bf16[1,128,2048]{2,1,0:T(8,128)(2,1)} custom-call(bf16[1,128,2048]{2,1,0:T(8,128)(2,1)} %signal_hbm.1, bf16[1,128,2048]{2,1,0:T(8,128)(2,1)} %gate_in_hbm.1, bf16[1,128,2048]{2,1,0:T(8,128)(2,1)} %gate_out_hbm.1, bf16[240,1024]{1,0:T(8,128)(2,1)} %constant.6.clone.features_hbm, f32[33,64]{1,0:T(8,128)} %pos_weight_hbm.1, f32[1,64]{1,0:T(1,128)} %bitcast.6, ...), custom_call_target="tpu_custom_call" | custom-call | tf_op jit(solution)/shard_map/hyena_layer/pallas_call | solution.py:466
  30.6 1.9 %copy.16 = bf16[1,128,2048]{2,1,0:T(8,128)(2,1)} copy(bf16[1,128,2048]{2,1,0:T(8,128)(2,1)} %hyena_layer.1) | data formatting | bytes 1048576

commit v6 on v5

--- a/solution.py
+++ b/solution.py
@@ -149,8 +149,8 @@
 def partner(me, mask, count):
     total, bit = 0, 1
     while bit < count:
-        digit = (me // bit) % 2
-        total = total + bit * ((1 - digit) if mask & bit else digit)
+        digit, flip = (me // bit) % 2, (mask // bit) % 2
+        total = total + bit * (digit + flip - 2 * digit * flip)
         bit *= 2
     return total
 
@@ -208,13 +208,15 @@
     me = lax.axis_index("seq")
     chunks = own // LANES
     length = blocks * span
-    masks = list(range(blocks - 1, 0, -1))
-    peers = {mask: partner(me, mask, blocks) for mask in masks}
+    far_first = list(range(blocks - 1, 0, -1))
+    near_first = far_first[blocks // 2 :] + far_first[: blocks // 2]
+    odd = lax.axis_index("grp") % 2
+    peers = [partner(me, a + (b - a) * odd, blocks) for a, b in zip(near_first, far_first)]
 
     barrier = pltpu.get_barrier_semaphore()
-    for mask in masks:
+    for peer in peers:
         pl.semaphore_signal(
-            barrier, inc=1, device_id={"seq": peers[mask]}, device_id_type=pl.DeviceIdType.MESH
+            barrier, inc=1, device_id={"seq": peer}, device_id_type=pl.DeviceIdType.MESH
         )
     mine = pl.ds(pl.multiple_of(me * own, LANES), own)
     pairs = [
@@ -252,17 +254,17 @@
         inbox[chunk, me] = gated[me, chunk]
 
     gate(0)
-    pl.semaphore_wait(barrier, len(masks))
+    pl.semaphore_wait(barrier, len(peers))
 
     def exchange(phase, chunk, source_of, target):
         copies = []
-        for mask in masks:
+        for slot, peer in enumerate(peers):
             copy = pltpu.make_async_remote_copy(
-                src_ref=source_of(peers[mask]),
+                src_ref=source_of(peer),
                 dst_ref=target.at[chunk, me],
-                send_sem=send_sem.at[phase, chunk, mask],
-                recv_sem=recv_sem.at[phase, chunk, mask],
-                device_id={"seq": peers[mask]},
+                send_sem=send_sem.at[phase, chunk, slot],
+                recv_sem=recv_sem.at[phase, chunk, slot],
+                device_id={"seq": peer},
                 device_id_type=pl.DeviceIdType.MESH,
             )
             copy.start()
@@ -411,9 +413,9 @@
     for chunk in range(chunks):
         finish(chunk, 0, me, outbox[chunk, me])
     for chunk in range(chunks):
-        for mask, copy in reversed(list(zip(masks, outgoing[chunk]))):
+        for slot, (peer, copy) in enumerate(zip(peers, outgoing[chunk])):
             copy.wait_recv()
-            finish(chunk, mask, peers[mask], returned[chunk, peers[mask]])
+            finish(chunk, slot + 1, peer, returned[chunk, peer])
     for copy in leaving:
         copy.wait()
     for copies in incoming[-1:] + outgoing:

time: 32.6 us -> 32.7 us (level)
  no operation moved by 1% of the time
where the time goes in v6:
time: 32.7 us; the launch traced here: 32.6 us
  Pallas kernels  30.7 us (94%)
  local copies, waits for them, and re-layouts  1.88 us (6%)
    pallas_call x1, Pallas kernels, fused(): pl.pallas_call(functools.partial(layer_kernel, blocks, span, own), out_sh...  30.7 us
    unnamed x1, local copies, waits for them, and re-layouts  1.88 us

profile of v6, /device:TPU:0, one launch (start us, length us, event | category | flops | bytes accessed | tf_op | source)
XLA Modules:
  0.0 32.6 jit_solution(12687071846133231988)
XLA Ops:
  0.0 30.7 %hyena_layer.1 = bf16[1,128,2048]{2,1,0:T(8,128)(2,1)} custom-call(bf16[1,128,2048]{2,1,0:T(8,128)(2,1)} %signal_hbm.1, bf16[1,128,2048]{2,1,0:T(8,128)(2,1)} %gate_in_hbm.1, bf16[1,128,2048]{2,1,0:T(8,128)(2,1)} %gate_out_hbm.1, bf16[240,1024]{1,0:T(8,128)(2,1)} %constant.6.clone.features_hbm, f32[33,64]{1,0:T(8,128)} %pos_weight_hbm.1, f32[1,64]{1,0:T(1,128)} %bitcast.6, ...), custom_call_target="tpu_custom_call" | custom-call | tf_op jit(solution)/shard_map/hyena_layer/pallas_call | solution.py:468
  30.7 1.9 %copy.16 = bf16[1,128,2048]{2,1,0:T(8,128)(2,1)} copy(bf16[1,128,2048]{2,1,0:T(8,128)(2,1)} %hyena_layer.1) | data formatting | bytes 1048576
